TPU v7x, 128 devices: a whole 4x4x4 slice. The times are simulated.
128 devices in a mesh: rep: 8 (over x, z_lo), blk: 16 (over y, z_hi, core).
Axes of the slice: x: 4, y: 4, z: 4 (z_hi: 2, z_lo: 2; z = z_hi * 2 + z_lo), core: 2. Of those that a mesh axis runs over, the one named last changes fastest.
Arguments:
- acts: bfloat16 [4096, 8192], P('rep', 'blk'), may hold values from -6 to 6
- out_grads: bfloat16 [4096, 1024], P('rep'), may hold values from -0.119628906 to 0.119628906
- codes: bfloat16 [8192, 8192], P('blk'), may hold values from -127 to 127, as said below
- scales: float32 [64, 64], P('blk')
- old_factor: float32 [8192, 8192], P('rep', 'blk'), may hold values from -0.12 to 0.12
- due: int32 [64, 64], P('rep', 'blk'), may hold values 0 or 1
Outputs:
- precond: bfloat16 [8192, 1024], P('blk')
- new_factor: float32 [8192, 8192], P('rep', 'blk')
Inputs may be any that keep to these rules, and one draw needn't show every extreme that they name: codes are whole numbers, and codes and scales are symmetric matrices.
All inputs are finite; a program needn't handle non-finite values. No bound on the sum of `due` on one device may be relied on, other than what follows from the above.
Results may differ from a plain program's by a relative error of at most 0.012.
Values may be sent and summed in bfloat16 or wider, within the bound.
A program may use at most 192 MiB of HBM per device.

v0:
```python
import jax
import jax.numpy as jnp
from jax import lax
from jax.sharding import PartitionSpec as P


def tdot(left, right):
    return lax.dot_general(
        left, right, (((0,), (0,)), ((), ())), preferred_element_type=jnp.float32
    )


def local(acts, out_grads, codes, scales, old_factor, due):
    partial_value = tdot(acts, out_grads)
    grad = lax.psum(partial_value, "rep").astype(jnp.bfloat16)
    whole = lax.all_gather(acts, "blk", axis=1, tiled=True)
    total = acts.shape[0] * lax.axis_size("rep")
    columns = whole
    stats = (
        lax.psum_scatter(
            tdot(columns, acts).astype(jnp.bfloat16), "rep", scatter_dimension=0, tiled=True
        ).astype(jnp.float32)
        / total
    )
    block = codes.shape[1] // scales.shape[1]
    mask_full = jnp.repeat(jnp.repeat(due, block, axis=0), block, axis=1)
    blend = 0.5 * old_factor + 0.5 * stats
    new_factor = jnp.where(mask_full == 1, blend, old_factor)
    scale_full = jnp.repeat(jnp.repeat(scales, block, axis=0), block, axis=1)
    inverse = (codes.astype(jnp.float32) * scale_full).astype(jnp.bfloat16)
    columns = inverse
    result = jnp.dot(
        columns, lax.all_gather(grad, "blk", axis=0, tiled=True), preferred_element_type=jnp.float32
    )
    precond = result.astype(jnp.bfloat16)
    return (precond, new_factor)


def solution(mesh):
    return jax.shard_map(
        local,
        mesh=mesh,
        in_specs=(
            P("rep", "blk"),
            P("rep", None),
            P("blk", None),
            P("blk", None),
            P("rep", "blk"),
            P("rep", "blk"),
        ),
        out_specs=(P("blk", None), P("rep", "blk")),
        check_vma=False,
    )
```

profile of v0, /device:TPU:1, one launch (start us, length us, event | category | flops | bytes accessed | tf_op | source)
XLA Modules:
  0.0 438.1 jit_solution(11022446042331841337)
XLA Ops:
  7.2 0.0 copy-start
  7.2 0.0 all-gather.5.cloned.1.call-start
  7.2 0.7 all-gather.5.cloned.1.call-update
  7.9 0.0 all-gather.3.cloned.1.call-start
  8.0 0.4 copy-done
  8.4 1.8 fusion.6
  10.2 113.2 %all-reduce.1 = bf16[512,1024]{1,0:T(8,128)(2,1)} all-reduce(f32[512,1024]{1,0:T(8,128)S(1)} %fusion.6), channel_id=1, replica_groups=mesh['rep'=8,'blk'=16] {'rep'}, use_global_device_ids=true, to_apply=%region_0.0 | all-reduce | flops 524288 | bytes 3145728 | tf_op jit(solution)/shard_map/psum | solution.py:15
  123.3 0.0 all-gather.3.cloned.1.call-update
  123.4 0.0 reduce-scatter.2.cloned.1.call-start
  123.4 19.8 %all-gather.5.cloned.1.call-done = bf16[512,8192]{1,0:T(8,128)(2,1)} async-done(((bf16[512,512]{1,0:T(8,128)(2,1)}), bf16[512,8192]{1,0:T(8,128)(2,1)}) %all-gather.5.cloned.1.call-update) | async-done | bytes 8388624 | tf_op jit(solution)/shard_map/all_gather | solution.py:16
  143.2 11.2 %convolution_convert_fusion = bf16[8192,512]{1,0:T(8,128)(2,1)} fusion(bf16[512,8192]{1,0:T(8,128)(2,1)} %all-gather.5.cloned.1.call-done, bf16[512,512]{1,0:T(8,128)(2,1)} %param.6), kind=kOutput, calls=%fused_computation.2 | convolution fusion | flops 4299161600 | bytes 17301504 | tf_op jit(solution)/shard_map/dot_general | solution.py:8
  154.4 0.0 copy-start.4
  154.4 0.0 reduce-scatter.2.cloned.1.call-update
  154.5 0.7 copy-done.4
  155.1 0.1 copy.8
  155.2 101.2 %all-gather.3.cloned.1.call-done = bf16[8192,1024]{1,0:T(8,128)(2,1)} async-done(((bf16[512,1024]{1,0:T(8,128)(2,1)}), bf16[8192,1024]{1,0:T(8,128)(2,1)}) %all-gather.3.cloned.1.call-update) | async-done | bytes 16777232 | tf_op jit(solution)/shard_map/all_gather | solution.py:33
  256.4 0.0 copy-done.3
  256.5 7.2 %broadcast_in_dim.13 = f32[512,64,128]{2,1,0:T(8,128)} broadcast(f32[512,64]{1,0:T(8,128)S(1)} %bitcast.20), dimensions={0,1} | broadcast | bytes 16908288 | tf_op jit(solution)/shard_map/broadcast_in_dim | solution.py:29
  263.7 29.2 %fusion.3 = bf16[512,1024]{1,0:T(8,128)(2,1)} fusion(bf16[8192,1024]{1,0:T(8,128)(2,1)} %all-gather.3.cloned.1.call-done, f32[64,8,64,128]{3,2,1,0:T(8,128)} %bitcast.18, bf16[512,8192]{1,0:T(8,128)(2,1)} %param.8), kind=kOutput, calls=%fused_computation.5 | convolution fusion | flops 8603041792 | bytes 42991616 | tf_op jit(solution)/shard_map/dot_general | solution.py:32
  292.8 132.4 %reduce-scatter.2.cloned.1.call-done = bf16[1024,512]{1,0:T(8,128)(2,1)} async-done(((bf16[8192,512]{1,0:T(8,128)(2,1)}), bf16[1024,512]{1,0:T(8,128)(2,1)}) %reduce-scatter.2.cloned.1.call-update) | async-done | bytes 1048592 | tf_op jit(solution)/shard_map/reduce_scatter | solution.py:20
  425.3 3.2 broadcast_in_dim.15
  428.5 0.0 copy-done.2
  428.5 3.1 add_select_fusion
  431.6 0.0 copy-done.1
  (6 shorter events, 0.1 us)
Async XLA Ops:
  7.2 1.2 copy-start
  7.2 136.1 %all-gather.5.cloned.1.call-start = ((), (), s32[]{:S(2)}) async-start(), calls=%async_computation.2 | async-start | bytes 8912896 | tf_op jit(solution)/shard_map/all_gather | solution.py:16
  7.9 248.5 %all-gather.3.cloned.1.call-start = ((), (), s32[]{:S(2)}) async-start(), calls=%async_computation.1 | async-start | bytes 17825792 | tf_op jit(solution)/shard_map/all_gather | solution.py:33
  123.4 301.9 %reduce-scatter.2.cloned.1.call-start = ((), (), s32[]{:S(2)}) async-start(), calls=%async_computation.3 | async-start | bytes 9437184 | tf_op jit(solution)/shard_map/reduce_scatter | solution.py:20
  154.4 0.7 copy-start.4
  154.4 102.0 %copy-start.3 = (f32[4,64]{1,0:T(4,128)S(1)}, f32[4,64]{1,0:T(4,128)}, u32[]{:S(2)}) copy-start(f32[4,64]{1,0:T(4,128)} %param.9) | copy-start | bytes 3076
  263.7 164.8 %copy-start.2 = (f32[1024,512]{1,0:T(8,128)S(1)}, f32[1024,512]{1,0:T(8,128)}, u32[]{:S(2)}) copy-start(f32[1024,512]{1,0:T(8,128)} %param.10) | copy-start | bytes 6291460
  263.7 167.9 %copy-start.1 = (bf16[512,1024]{1,0:T(8,128)(2,1)S(1)}, bf16[512,1024]{1,0:T(8,128)(2,1)}, u32[]{:S(2)}) copy-start(bf16[512,1024]{1,0:T(8,128)(2,1)} %param.7) | copy-start | bytes 3145732
Sparse Core Ops, SparseCore 0:
  10.3 132.9 all-gather.4
  146.2 110.1 all-gather.2
  258.8 166.3 reduce-scatter.1
where the time goes:
time: 438 us
  waiting for transfers between devices  254 us (58%)
  blocking collectives  113 us (26%)
  matrix products  42.1 us (10%)
  between operations  13.8 us (3%)
  local copies, waits for them, and re-layouts  11.6 us (3%)
    reduce_scatter x1, waiting for transfers between devices, local(): lax.psum_scatter(tdot(columns, acts).astype(jnp.bfloat16), 'rep', scatter...  132 us
    psum x1, blocking collectives, local(): grad = lax.psum(partial_value, 'rep').astype(jnp.bfloat16)  113 us
    all_gather x1, waiting for transfers between devices, local(): lax.all_gather(grad, 'blk', axis=0, tiled=True)  101 us
    dot_general x1, matrix products, local(): jnp.dot(columns, lax.all_gather(grad, 'blk', axis=0, tiled=True), preferr...  29.2 us
    all_gather x1, waiting for transfers between devices, local(): whole = lax.all_gather(acts, 'blk', axis=1, tiled=True)  19.8 us
    dot_general x2, matrix products, tdot(): lax.dot_general(left, right, (((0,), (0,)), ((), ())), preferred_element_...  13 us
  transfers between devices with their start and end apart: 3, of which 3 were waited for; matrix products, arithmetic and copies ran while one was open for 11% of the time, Pallas kernels for 0%

commit v1 on v0

v1 whole, which is shorter than its diff:
```python
import functools

import jax
import jax.numpy as jnp
from jax import lax
from jax.experimental import pallas as pl
from jax.experimental.pallas import tpu as pltpu
from jax.sharding import PartitionSpec as P

MESH = pl.DeviceIdType.MESH
F32, BF16 = jnp.float32, jnp.bfloat16


def tdot(left, right):
    return lax.dot_general(
        left, right, (((0,), (0,)), ((), ())), preferred_element_type=F32
    )


def kernel(
    acts, out_grads, codes, scales, old_factor, due, precond, new_factor,
    cols, rows, spread, band, partial, parts, grad, inverse, factor, stats, piece,
    send, recv, local,
):
    r, b = lax.axis_index("rep"), lax.axis_index("blk")
    x, zl = r // 2, r % 2
    y, zh, k = b // 4, (b // 2) % 2, b % 2
    z = 2 * zh + zl
    turned = 2 * zl + zh

    def device(x, y, z, k):
        return (2 * (x % 4) + z % 2, 4 * (y % 4) + 2 * (z // 2) + k)

    def along_x(step, flip=0):
        return device(x + step, y, 2 * zh + (1 - zl if flip else zl), k)

    def along_y(step):
        return device(x, y + step, z, k)

    zl_mate = along_x(0, 1)
    zh_mate = device(x, y, 2 * (1 - zh) + zl, k)
    sibling = device(x, y, z, 1 - k)

    count = [0, 0]
    started = []

    def put(src, dst, target, start=True):
        i = count[0]
        count[0] += 1
        copy = pltpu.make_async_remote_copy(
            src_ref=src, dst_ref=dst, send_sem=send.at[i], recv_sem=recv.at[i],
            device_id=target, device_id_type=MESH,
        )
        copy.start()
        started.append(copy)
        return copy

    def bring(src, dst):
        i = count[1]
        count[1] += 1
        copy = pltpu.make_async_copy(src, dst, local.at[i])
        copy.start()
        return copy

    get_acts = bring(acts, cols.at[x, zl])
    get_band = bring(out_grads, band)
    get_codes = [bring(codes.at[:, pl.ds(512 * i, 512)], inverse.at[i]) for i in range(16)]
    get_old = bring(old_factor, factor)

    barrier = pltpu.get_barrier_semaphore()
    partners = [along_x(step, flip) for flip in (0, 1) for step in range(4) if step or flip]
    partners += [along_y(step) for step in (1, 2, 3)] + [zh_mate, sibling]
    for partner in partners:
        pl.semaphore_signal(barrier, inc=1, device_id=partner, device_id_type=MESH)
    mixed = zl != zh

    @pl.when(mixed)
    def _():
        for step in range(4):
            pl.semaphore_signal(
                barrier, inc=1, device_id=device(x + step, y, turned, k), device_id_type=MESH
            )

    get_acts.wait()
    get_band.wait()
    mine = cols[x, zl].reshape(512, 512)
    for i in range(4):
        part = tdot(mine, band[:, 256 * i : 256 * i + 256]).astype(BF16)
        partial[2 * i] = part[:, :128]
        partial[2 * i + 1] = part[:, 128:]

    pl.semaphore_wait(barrier, len(partners) + 4 * (zl + zh - 2 * zl * zh))

    scatter = []
    for step, flip in ((1, 0), (3, 0), (0, 1), (1, 1), (3, 1), (2, 0), (2, 1)):
        to = 2 * ((x + step) % 4) + (1 - zl if flip else zl)
        scatter.append(put(partial.at[to], parts.at[r], along_x(step, flip)))

    spread_sends = [
        put(cols.at[x, zl, (y + step) % 4], spread.at[y], along_y(step)) for step in (1, 3, 2)
    ]
    own_quarter = bring(cols.at[x, zl, y], spread.at[y])
    cols_zl = put(cols.at[x, zl], cols.at[x, zl], zl_mate)

    stats[...] = jnp.zeros_like(stats)

    def dequantize(i):
        for u in range(4):
            for v in range(4):
                at = (i, pl.ds(128 * u, 128), pl.ds(128 * v, 128))
                inverse[at] = (inverse[at].astype(F32) * scales[u, 4 * i + v]).astype(BF16)

    def dequantize_some(first, last):
        for i in range(first, last):
            get_codes[i].wait()
        lax.fori_loop(first, last, lambda i, c: (dequantize(i), c)[1], 0)

    dequantize_some(0, 8)

    own_quarter.wait()
    for copy in spread_sends:
        copy.wait_recv()
    turns = []
    for step in (1, 3, 2):
        to = (x + step) % 4
        turns.append(put(spread.at[to], rows.at[k, x, zl, y], device(to, y, turned, k)))
    i0 = count[0]
    count[0] += 1
    stay = pltpu.make_async_copy(spread.at[x], rows.at[k, x, zl, y], recv.at[i0])
    go = pltpu.make_async_remote_copy(
        src_ref=spread.at[x], dst_ref=rows.at[k, x, zl, y], send_sem=send.at[i0],
        recv_sem=recv.at[i0], device_id=device(x, y, turned, k), device_id_type=MESH,
    )

    @pl.when(mixed)
    def _():
        go.start()

    @pl.when(jnp.logical_not(mixed))
    def _():
        stay.start()

    dequantize_some(8, 16)

    for copy in scatter:
        copy.wait_recv()
    total = partial[r].astype(F32)
    for step, flip in ((1, 0), (3, 0), (0, 1), (1, 1), (3, 1), (2, 0), (2, 1)):
        frm = 2 * ((x + step) % 4) + (1 - zl if flip else zl)
        total = total + parts[frm].astype(F32)
    grad[y, zh, k] = total.astype(BF16)
    own = grad.at[y, zh, k]
    other = grad.at[y, 1 - zh, k]
    grad_zh = put(own, own, zh_mate)
    grad_own = {step: put(own, own, along_y(step)) for step in (1, 3, 2)}

    def half(ref, h):
        return ref.at[pl.ds(2 * h, 2)]

    def both_ways(ref, plus, minus):
        sends = {}
        for h in (0, 1):
            part = half(ref, h)
            sends[1, h] = put(part, part, plus)
            sends[3, h] = put(part, part, minus)
        return sends

    cols_own = both_ways(cols.at[x, zl], along_x(1), along_x(3))

    for copy in turns:
        copy.wait_recv()
    stay.wait()

    def group(zl_of, q, h=None):
        if h is None:
            return rows.at[k, :, zl_of, q]
        return rows.at[k, pl.ds(2 * h, 2), zl_of, q]

    rows_zh = [put(group(zh, y, h), group(zh, y, h), zh_mate) for h in (0, 1)]

    def along_both(zl_of):
        sends = {}
        for h in (0, 1):
            part = group(zl_of, y, h)
            sends[1, h] = put(part, part, along_y(1))
            sends[3, h] = put(part, part, along_y(3))
        return sends

    rows_a = along_both(zh)
    share = [put(group(zh, y), group(zh, y), sibling)]

    grad_zh.wait_recv()
    grad_other = {step: put(other, other, along_y(step)) for step in (1, 3, 2)}
    pair = grad.at[y, :, k]
    grad_share = [put(pair, pair, sibling)]

    cols_zl.wait_recv()
    cols_other = both_ways(cols.at[x, 1 - zl], along_x(1), along_x(3))

    for copy in rows_zh:
        copy.wait_recv()
    rows_b = along_both(1 - zh)
    share.append(put(group(1 - zh, y), group(1 - zh, y), sibling))

    for step in (1, 3, 2):
        grad_own[step].wait_recv()
        grad_other[step].wait_recv()
        pair = grad.at[(y - step + 4) % 4, :, k]
        grad_share.append(put(pair, pair, sibling))

    def forward_rows(sends, zl_of):
        sends[1, 0].wait_recv()
        low = group(zl_of, (y + 3) % 4, 0)
        forth = put(low, low, along_y(1))
        sends[3, 1].wait_recv()
        high = group(zl_of, (y + 1) % 4, 1)
        back = put(high, high, along_y(3))
        return forth, back

    def forward_cols(sends, zl_of):
        sends[1, 0].wait_recv()
        low = half(cols.at[(x + 3) % 4, zl_of], 0)
        forth = put(low, low, along_x(1))
        sends[3, 1].wait_recv()
        high = half(cols.at[(x + 1) % 4, zl_of], 1)
        back = put(high, high, along_x(3))
        return forth, back

    far_cols_own = forward_cols(cols_own, zl)
    far_rows_a = forward_rows(rows_a, zh)

    result = jnp.zeros((512, 128), F32)
    for copy in grad_share:
        copy.wait_recv()

    def add(i, total):
        return total + jnp.dot(
            inverse[i], grad[i // 4, (i // 2) % 2, i % 2], preferred_element_type=F32
        )

    piece[...] = lax.fori_loop(0, 16, add, result).astype(BF16)

    def slot(of):
        return precond.at[:, pl.ds(pl.multiple_of(128 * of, 128), 128)]

    keep = bring(piece, slot(r))
    out_zl = put(piece, slot(r), zl_mate)
    out_own = [put(piece, slot(r), along_x(step)) for step in (1, 3, 2)]

    def share_rows(zl_of, q):
        share.append(put(group(zl_of, q), group(zl_of, q), sibling))

    def sides(sends, zl_of):
        sends[1, 1].wait_recv()
        share_rows(zl_of, (y + 3) % 4)
        sends[3, 0].wait_recv()
        share_rows(zl_of, (y + 1) % 4)

    sides(rows_a, zh)
    far_cols_other = forward_cols(cols_other, 1 - zl)
    far_rows_b = forward_rows(rows_b, 1 - zh)

    out_zl.wait_recv()
    mate = 2 * x + 1 - zl
    out_other = [put(slot(mate), slot(mate), along_x(step)) for step in (1, 3, 2)]

    for copy in far_rows_a:
        copy.wait_recv()
    share_rows(zh, (y + 2) % 4)
    sides(rows_b, 1 - zh)
    for copy in far_rows_b:
        copy.wait_recv()
    share_rows(1 - zh, (y + 2) % 4)

    for sends, far in ((cols_own, far_cols_own), (cols_other, far_cols_other)):
        sends[1, 1].wait_recv()
        sends[3, 0].wait_recv()
        for copy in far:
            copy.wait_recv()
    for copy in share:
        copy.wait_recv()

    def accumulate(i, c):
        kk, zz, q = i // 8, (i // 4) % 2, i % 4
        stats[kk] += tdot(
            rows[kk, :, zz, q].reshape(512, 512), cols[:, zz, q].reshape(512, 512)
        )
        return c

    lax.fori_loop(0, 16, accumulate, 0)

    get_old.wait()
    for i in range(8):
        for j in range(4):
            at = (pl.ds(128 * i, 128), pl.ds(128 * j, 128))
            old = factor[at]
            new = stats[i // 4, pl.ds(128 * (i % 4), 128), pl.ds(128 * j, 128)]
            blend = 0.5 * old + 0.5 * (new / 4096)
            factor[at] = jnp.where(due[i, j] == 1, blend, old)
    leave = bring(factor, new_factor)

    for copy in out_own + out_other:
        copy.wait_recv()
    for copy in started:
        copy.wait_send()

    @pl.when(mixed)
    def _():
        go.wait_send()

    keep.wait()
    leave.wait()


def local(acts, out_grads, codes, scales, old_factor, due):
    anywhere = pl.BlockSpec(memory_space=pl.ANY)
    scalar = pl.BlockSpec(memory_space=pltpu.SMEM)
    return pl.pallas_call(
        kernel,
        out_shape=(
            jax.ShapeDtypeStruct((512, 1024), BF16),
            jax.ShapeDtypeStruct((1024, 512), F32),
        ),
        in_specs=[anywhere, anywhere, anywhere, scalar, anywhere, scalar],
        out_specs=(anywhere, anywhere),
        scratch_shapes=[
            pltpu.VMEM((4, 2, 4, 128, 512), BF16),
            pltpu.VMEM((2, 4, 2, 4, 128, 512), BF16),
            pltpu.VMEM((4, 128, 512), BF16),
            pltpu.VMEM((512, 1024), BF16),
            pltpu.VMEM((8, 512, 128), BF16),
            pltpu.VMEM((8, 512, 128), BF16),
            pltpu.VMEM((4, 2, 2, 512, 128), BF16),
            pltpu.VMEM((16, 512, 512), BF16),
            pltpu.VMEM((1024, 512), F32),
            pltpu.VMEM((2, 512, 512), F32),
            pltpu.VMEM((512, 128), BF16),
            pltpu.SemaphoreType.DMA((80,)),
            pltpu.SemaphoreType.DMA((80,)),
            pltpu.SemaphoreType.DMA((24,)),
        ],
        compiler_params=pltpu.CompilerParams(
            collective_id=0, has_side_effects=True, vmem_limit_bytes=56 * 2**20
        ),
    )(acts.reshape(4, 128, 512), out_grads, codes, scales, old_factor, due)


def solution(mesh):
    return jax.shard_map(
        local,
        mesh=mesh,
        in_specs=(
            P("rep", "blk"),
            P("rep", None),
            P("blk", None),
            P("blk", None),
            P("rep", "blk"),
            P("rep", "blk"),
        ),
        out_specs=(P("blk", None), P("rep", "blk")),
        check_vma=False,
    )
```

time: 438 us -> 90.8 us (0.21)
  waiting for transfers between devices: 254 us -> 0 us
  blocking collectives: 113 us -> 0 us
  Pallas kernels: 0 us -> 84.9 us
  matrix products: 42.1 us -> 0 us
  between operations: 13.8 us -> 0.65 us
  local copies, waits for them, and re-layouts: 11.6 us -> 5.08 us
    reduce_scatter x1 -> x0, waiting for transfers between devices: 132 us -> none  [local(): lax.psum_scatter(tdot(columns, acts).astype(jnp.bfloat16), 'rep', scatter...]
    all_gather x2 -> x0, waiting for transfers between devices: 121 us -> none  [the longest x1 101 us: local(): lax.all_gather(grad, 'blk', axis=0, tiled=True)]
    psum x1 -> x0, blocking collectives: 113 us -> none  [local(): grad = lax.psum(partial_value, 'rep').astype(jnp.bfloat16)]
    pallas_call x0 -> x1, Pallas kernels: none -> 84.9 us  [local(): pl.pallas_call(kernel, out_shape=(jax.ShapeDtypeStruct((512, 1024), BF16)...]
    dot_general x3 -> x0, matrix products: 42.1 us -> none  [the longest x1 29.2 us: local(): jnp.dot(columns, lax.all_gather(grad, 'blk', axis=0, tiled=True), preferr...]
    broadcast_in_dim x4 -> x0, local copies, waits for them, and re-layouts: 10.4 us -> none  [the longest x2 7.22 us: local(): scale_full = jnp.repeat(jnp.repeat(scales, block, axis=0), block, axis=1)]
  transfers between devices with their start and end apart: 3 -> 0, of which waited for: 3 -> 0; matrix products, arithmetic and copies ran while one was open for 11% -> 0% of each run, Pallas kernels for 0% -> 0%
where the time goes in v1:
time: 90.8 us; the launch traced here: 90.7 us
  Pallas kernels  84.9 us (94%)
  local copies, waits for them, and re-layouts  5.08 us (6%)
    pallas_call x1, Pallas kernels, local(): pl.pallas_call(kernel, out_shape=(jax.ShapeDtypeStruct((512, 1024), BF16)...  84.9 us
    unnamed x5, local copies, waits for them, and re-layouts  5.08 us

profile of v1, /device:TPU:1, one launch (start us, length us, event | category | flops | bytes accessed | tf_op | source)
XLA Modules:
  0.0 90.7 jit_solution(13283800899790920070)
XLA Ops:
  0.6 1.3 %copy.8.due = s32[8,4]{1,0:T(8,128)} copy(s32[8,4]{0,1:T(4,128)} %param.11) | data formatting | bytes 256 | tf_op args[5]
  2.0 84.9 %shard_map.77 = (bf16[512,1024]{1,0:T(8,128)(2,1)}, f32[1024,512]{1,0:T(8,128)}) custom-call(bf16[4,128,512]{2,1,0:T(8,128)(2,1)} %bitcast.1, bf16[512,1024]{1,0:T(8,128)(2,1)} %out_grads.1, bf16[512,8192]{1,0:T(8,128)(2,1)} %codes.1, f32[4,64]{1,0:T(4,128)} %scales.1, f32[1024,512]{1,0:T(8,128)} %old_factor.1, s32[8,4]{1,0:T(8,128)} %copy.8.due), custom_call_target="tpu_custom_call" | custom-call | tf_op jit(solution)/shard_map/pallas_call | solution.py:318
  86.9 0.0 copy-start
  86.9 2.4 %copy.11 = bf16[512,1024]{1,0:T(8,128)(2,1)} copy(bf16[512,1024]{1,0:T(8,128)(2,1)} %get-tuple-element.4) | data formatting | bytes 2097152
  89.3 0.0 copy-done
  89.3 1.3 %copy.12 = f32[1024,512]{1,0:T(8,128)} copy(f32[1024,512]{1,0:T(8,128)S(1)} %copy-done) | data formatting | bytes 4194304
Async XLA Ops:
  86.9 2.4 %copy-start = (f32[1024,512]{1,0:T(8,128)S(1)}, f32[1024,512]{1,0:T(8,128)}, u32[]{:S(2)}) copy-start(f32[1024,512]{1,0:T(8,128)} %get-tuple-element.5) | copy-start | bytes 6291460

commit v2 on v0

v2 whole, which is shorter than its diff:
```python
import jax
import jax.numpy as jnp
from jax import lax
from jax.experimental import pallas as pl
from jax.experimental.pallas import tpu as pltpu
from jax.sharding import PartitionSpec as P

MESH = pl.DeviceIdType.MESH
F32, BF16 = jnp.float32, jnp.bfloat16


def tdot(left, right):
    return lax.dot_general(
        left, right, (((0,), (0,)), ((), ())), preferred_element_type=F32
    )


def kernel(
    acts, out_grads, codes, scales, old_factor, due, precond, new_factor,
    cols, rows, spread, band, partial, parts, grad, inverse, factor, stats, piece,
    send, recv, local,
):
    r, b = lax.axis_index("rep"), lax.axis_index("blk")
    x, zl = r // 2, r % 2
    y, zh, k = b // 4, (b // 2) % 2, b % 2
    z = 2 * zh + zl
    turned = 2 * zl + zh
    mixed = zl != zh

    def device(x, y, z, k):
        return (2 * (x % 4) + z % 2, 4 * (y % 4) + 2 * (z // 2) + k)

    def along_x(step, flip=0):
        return device(x + step, y, 2 * zh + (1 - zl if flip else zl), k)

    def along_y(step):
        return device(x, y + step, z, k)

    def xs(step):
        return (x + step) % 4

    def ys(step):
        return (y + step) % 4

    zl_mate = device(x, y, 2 * zh + 1 - zl, k)
    zh_mate = device(x, y, 2 * (1 - zh) + zl, k)
    sibling = device(x, y, z, 1 - k)

    count = [0, 0]
    sent = []

    def put(src, target, dst=None):
        i = count[0]
        count[0] += 1
        copy = pltpu.make_async_remote_copy(
            src_ref=src, dst_ref=src if dst is None else dst, send_sem=send.at[i],
            recv_sem=recv.at[i], device_id=target, device_id_type=MESH,
        )
        copy.start()
        sent.append(copy)
        return copy

    def bring(src, dst):
        i = count[1]
        count[1] += 1
        copy = pltpu.make_async_copy(src, dst, local.at[i])
        copy.start()
        return copy

    get_acts = bring(acts, cols.at[x, zl])
    get_band = bring(out_grads, band)
    get_codes = [bring(codes.at[:, pl.ds(512 * i, 512)], inverse.at[i]) for i in range(16)]
    get_old = bring(old_factor, factor)

    barrier = pltpu.get_barrier_semaphore()
    partners = [along_x(step, flip) for flip in (0, 1) for step in range(4) if step or flip]
    partners += [along_y(step) for step in (1, 2, 3)] + [zh_mate, sibling]
    for partner in partners:
        pl.semaphore_signal(barrier, inc=1, device_id=partner, device_id_type=MESH)

    @pl.when(mixed)
    def _():
        for step in range(4):
            pl.semaphore_signal(
                barrier, inc=1, device_id=device(x + step, y, turned, k), device_id_type=MESH
            )

    pl.semaphore_wait(barrier, len(partners) + 4 * (zl + zh - 2 * zl * zh))

    s = {}

    def spread_y():
        for step in (1, 3, 2):
            s["spread", step] = put(acts.at[ys(step)], along_y(step), spread.at[y])

    def put_or_keep(src, dst, target, stay, i, j):
        go = pltpu.make_async_remote_copy(
            src_ref=src, dst_ref=dst, send_sem=send.at[i], recv_sem=recv.at[j],
            device_id=target, device_id_type=MESH,
        )

        @pl.when(stay)
        def _():
            pltpu.make_async_copy(src, dst, recv.at[j]).start()

        @pl.when(jnp.logical_not(stay))
        def _():
            go.start()

        maybe.append((go, stay))

    def arrived(at, j):
        pltpu.make_async_copy(at, at, recv.at[j]).wait()

    maybe = []
    turn_base = 100

    def turn(step):
        to = ys(-step)
        if step:
            s["spread", step].wait_recv()
            src = spread.at[to]
        else:
            src = acts.at[y]
        stay = jnp.logical_and(to == x, jnp.logical_not(mixed))
        put_or_keep(
            src, rows.at[k, x, zl, y], device(to, y, turned, k), stay,
            turn_base + step, turn_base + x,
        )

    def group(which, q, h=None):
        zl_of = 1 - zh if which else zh
        if h is None:
            return rows.at[k, :, zl_of, q]
        return rows.at[k, pl.ds(2 * h, 2), zl_of, q]

    def rows_y(which, h):
        at = group(which, y, h)
        if which:
            s["rows_z", h].wait_recv()
        else:
            for i in (2 * h, 2 * h + 1):
                arrived(rows.at[k, i, zh, y], turn_base + i)
            s["rows_z", h] = put(at, zh_mate)
        s["rows", which, 1, h] = put(at, along_y(1))
        s["rows", which, 3, h] = put(at, along_y(3))

    def rows_far(which, step):
        h = 0 if step == 1 else 1
        s["rows", which, step, h].wait_recv()
        s["far", which, step] = put(group(which, ys(-step), h), along_y(step))

    def rows_share(which, step):
        if step == 0:
            pass
        elif step == 2:
            s["far", which, 1].wait_recv()
            s["far", which, 3].wait_recv()
        else:
            s["rows", which, step, 0 if step == 3 else 1].wait_recv()
        at = group(which, ys(-step))
        s["share", which, step] = put(at, sibling)

    def dot(own, which, step):
        kk = k if own else 1 - k
        zl_of = 1 - zh if which else zh
        if not own:
            s["share", which, step].wait_recv()
        q = ys(-step)
        stats[kk] += tdot(
            rows[kk, :, zl_of, q].reshape(512, 512), cols[:, zl_of, q].reshape(512, 512)
        )

    def cols_half(which, step, h):
        return cols.at[xs(step), 1 - zl if which else zl, pl.ds(2 * h, 2)]

    def cols_z():
        s["cols_z"] = put(cols.at[x, zl], zl_mate)

    def cols_x(which, h):
        if which and h == 0:
            s["cols_z"].wait_recv()
        at = cols_half(which, 0, h)
        s["cols", which, 1, h] = put(at, along_x(1))
        s["cols", which, 3, h] = put(at, along_x(3))

    def cols_far(step, which=0):
        h = 0 if step == 1 else 1
        s["cols", which, step, h].wait_recv()
        s["cols_far", which, step] = put(cols_half(which, -step, h), along_x(step))

    def cols_all():
        for which in (0, 1):
            s["cols", which, 1, 1].wait_recv()
            s["cols", which, 3, 0].wait_recv()
            s["cols_far", which, 1].wait_recv()
            s["cols_far", which, 3].wait_recv()

    def part_sum():
        get_acts.wait()
        get_band.wait()
        mine = cols[x, zl].reshape(512, 512)
        for i in range(4):
            part = tdot(mine, band[:, 256 * i : 256 * i + 256]).astype(BF16)
            partial[2 * i] = part[:, :128]
            partial[2 * i + 1] = part[:, 128:]

    def rep_of(step, flip):
        return 2 * xs(step) + (1 - zl if flip else zl)

    def part(step, flip):
        s["part", step, flip] = put(
            partial.at[rep_of(step, flip)], along_x(step, flip), parts.at[r]
        )

    def grad_sum():
        total = partial[r].astype(F32)
        for step, flip in ((1, 0), (3, 0), (0, 1), (1, 1), (3, 1), (2, 0), (2, 1)):
            s["part", step, flip].wait_recv()
            total = total + parts[rep_of(-step, flip)].astype(F32)
        grad[y, zh, k] = total.astype(BF16)
        at = grad.at[y, zh, k]
        s["grad_z"] = put(at, zh_mate)
        for step in (1, 3, 2):
            s["grad", 0, step] = put(at, along_y(step))

    def grad_other():
        s["grad_z"].wait_recv()
        at = grad.at[y, 1 - zh, k]
        for step in (1, 3, 2):
            s["grad", 1, step] = put(at, along_y(step))
        at = grad.at[y, :, k]
        s["grad_share", 0] = put(at, sibling)

    def grad_share(step):
        s["grad", 0, step].wait_recv()
        s["grad", 1, step].wait_recv()
        at = grad.at[ys(-step), :, k]
        s["grad_share", step] = put(at, sibling)

    def slot(of):
        return precond.at[:, pl.ds(pl.multiple_of(128 * of, 128), 128)]

    def result():
        for i in range(4):
            s["grad_share", i].wait_recv()

        def add(i, total):
            return total + jnp.dot(
                inverse[i], grad[i // 4, (i // 2) % 2, i % 2], preferred_element_type=F32
            )

        piece[...] = lax.fori_loop(0, 16, add, jnp.zeros((512, 128), F32)).astype(BF16)
        s["keep"] = bring(piece, slot(r))
        s["out_z"] = put(piece, zl_mate, slot(r))
        for step in (1, 3, 2):
            s["out", 0, step] = put(piece, along_x(step), slot(r))

    def result_other():
        s["out_z"].wait_recv()
        at = slot(2 * x + 1 - zl)
        for step in (1, 3, 2):
            s["out", 1, step] = put(at, along_x(step))

    def result_end():
        for which in (0, 1):
            for step in (1, 3, 2):
                s["out", which, step].wait_recv()

    def dequantize(first, last):
        for i in range(first, last):
            get_codes[i].wait()

        def block(i, c):
            for u in range(4):
                for v in range(4):
                    at = (i, pl.ds(128 * u, 128), pl.ds(128 * v, 128))
                    inverse[at] = (inverse[at].astype(F32) * scales[u, 4 * i + v]).astype(BF16)
            return c

        lax.fori_loop(first, last, block, 0)

    def clear():
        stats[...] = jnp.zeros_like(stats)

    def blend(own):
        kk = k if own else 1 - k
        if own:
            get_old.wait()
        for i in range(4):
            for j in range(4):
                at = (pl.ds(512 * kk + 128 * i, 128), pl.ds(128 * j, 128))
                old = factor[at]
                new = stats[kk, pl.ds(128 * i, 128), pl.ds(128 * j, 128)]
                mixture = 0.5 * old + 0.5 * (new / 4096)
                factor[at] = jnp.where(due[j, 4 * kk + i] == 1, mixture, old)
        at = pl.ds(512 * kk, 512)
        s["leave", own] = bring(factor.at[at], new_factor.at[at])

    part_sum()
    part(1, 0)
    part(3, 0)
    part(0, 1)
    part(1, 1)
    part(3, 1)
    part(2, 0)
    part(2, 1)
    spread_y()
    cols_z()
    clear()
    dequantize(0, 8)
    turn(1)
    turn(3)
    turn(2)
    turn(0)
    dequantize(8, 16)
    grad_sum()
    cols_x(0, 0)
    cols_x(0, 1)
    rows_y(0, 0)
    rows_y(0, 1)
    rows_share(0, 0)
    grad_other()
    cols_x(1, 0)
    cols_x(1, 1)
    rows_y(1, 0)
    rows_y(1, 1)
    rows_share(1, 0)
    grad_share(1)
    grad_share(3)
    grad_share(2)
    cols_far(1)
    cols_far(3)
    rows_far(0, 1)
    rows_far(0, 3)
    result()
    rows_share(0, 1)
    rows_share(0, 3)
    cols_far(1, 1)
    cols_far(3, 1)
    rows_far(1, 1)
    rows_far(1, 3)
    result_other()
    rows_share(0, 2)
    rows_share(1, 1)
    rows_share(1, 3)
    cols_all()
    for which, step in ((0, 0), (1, 0), (0, 1), (0, 3), (0, 2), (1, 1), (1, 3)):
        dot(1, which, step)
        dot(0, which, step)
    rows_share(1, 2)
    dot(1, 1, 2)
    blend(1)
    dot(0, 1, 2)
    blend(0)
    result_end()

    for copy in sent:
        copy.wait_send()
    for go, stay in maybe:

        @pl.when(jnp.logical_not(stay))
        def _():
            go.wait_send()

    s["keep"].wait()
    s["leave", 1].wait()
    s["leave", 0].wait()


def local(acts, out_grads, codes, scales, old_factor, due):
    anywhere = pl.BlockSpec(memory_space=pl.ANY)
    scalar = pl.BlockSpec(memory_space=pltpu.SMEM)
    return pl.pallas_call(
        kernel,
        out_shape=(
            jax.ShapeDtypeStruct((512, 1024), BF16),
            jax.ShapeDtypeStruct((1024, 512), F32),
        ),
        in_specs=[anywhere, anywhere, anywhere, scalar, anywhere, scalar],
        out_specs=(anywhere, anywhere),
        scratch_shapes=[
            pltpu.VMEM((4, 2, 4, 128, 512), BF16),
            pltpu.VMEM((2, 4, 2, 4, 128, 512), BF16),
            pltpu.VMEM((4, 128, 512), BF16),
            pltpu.VMEM((512, 1024), BF16),
            pltpu.VMEM((8, 512, 128), BF16),
            pltpu.VMEM((8, 512, 128), BF16),
            pltpu.VMEM((4, 2, 2, 512, 128), BF16),
            pltpu.VMEM((16, 512, 512), BF16),
            pltpu.VMEM((1024, 512), F32),
            pltpu.VMEM((2, 512, 512), F32),
            pltpu.VMEM((512, 128), BF16),
            pltpu.SemaphoreType.DMA((104,)),
            pltpu.SemaphoreType.DMA((104,)),
            pltpu.SemaphoreType.DMA((24,)),
        ],
        compiler_params=pltpu.CompilerParams(
            collective_id=0, has_side_effects=True, vmem_limit_bytes=56 * 2**20
        ),
    )(acts.reshape(4, 128, 512), out_grads, codes, scales, old_factor, due.T)


def solution(mesh):
    return jax.shard_map(
        local,
        mesh=mesh,
        in_specs=(
            P("rep", "blk"),
            P("rep", None),
            P("blk", None),
            P("blk", None),
            P("rep", "blk"),
            P("rep", "blk"),
        ),
        out_specs=(P("blk", None), P("rep", "blk")),
        check_vma=False,
    )
```

time: 438 us -> 87.2 us (0.20)
  waiting for transfers between devices: 254 us -> 0 us
  blocking collectives: 113 us -> 0 us
  Pallas kernels: 0 us -> 82.7 us
  matrix products: 42.1 us -> 0 us
  between operations: 13.8 us -> 0.65 us
  local copies, waits for them, and re-layouts: 11.6 us -> 3.73 us
    reduce_scatter x1 -> x0, waiting for transfers between devices: 132 us -> none  [local(): lax.psum_scatter(tdot(columns, acts).astype(jnp.bfloat16), 'rep', scatter...]
    all_gather x2 -> x0, waiting for transfers between devices: 121 us -> none  [the longest x1 101 us: local(): lax.all_gather(grad, 'blk', axis=0, tiled=True)]
    psum x1 -> x0, blocking collectives: 113 us -> none  [local(): grad = lax.psum(partial_value, 'rep').astype(jnp.bfloat16)]
    pallas_call x0 -> x1, Pallas kernels: none -> 82.7 us  [local(): pl.pallas_call(kernel, out_shape=(jax.ShapeDtypeStruct((512, 1024), BF16)...]
    dot_general x3 -> x0, matrix products: 42.1 us -> none  [the longest x1 29.2 us: local(): jnp.dot(columns, lax.all_gather(grad, 'blk', axis=0, tiled=True), preferr...]
    broadcast_in_dim x4 -> x0, local copies, waits for them, and re-layouts: 10.4 us -> none  [the longest x2 7.22 us: local(): scale_full = jnp.repeat(jnp.repeat(scales, block, axis=0), block, axis=1)]
  transfers between devices with their start and end apart: 3 -> 0, of which waited for: 3 -> 0; matrix products, arithmetic and copies ran while one was open for 11% -> 0% of each run, Pallas kernels for 0% -> 0%
where the time goes in v2:
time: 87.2 us; the launch traced here: 87.1 us
  Pallas kernels  82.7 us (95%)
  local copies, waits for them, and re-layouts  3.73 us (4%)
    pallas_call x1, Pallas kernels, local(): pl.pallas_call(kernel, out_shape=(jax.ShapeDtypeStruct((512, 1024), BF16)...  82.7 us
    unnamed x4, local copies, waits for them, and re-layouts  3.73 us

profile of v2, /device:TPU:1, one launch (start us, length us, event | category | flops | bytes accessed | tf_op | source)
XLA Modules:
  0.0 87.1 jit_solution(10335111460011713318)
XLA Ops:
  0.6 82.7 %shard_map.77 = (bf16[512,1024]{1,0:T(8,128)(2,1)}, f32[1024,512]{1,0:T(8,128)}) custom-call(bf16[4,128,512]{2,1,0:T(8,128)(2,1)} %bitcast.2, bf16[512,1024]{1,0:T(8,128)(2,1)} %out_grads.1, bf16[512,8192]{1,0:T(8,128)(2,1)} %codes.1, f32[4,64]{1,0:T(4,128)} %scales.1, f32[1024,512]{1,0:T(8,128)} %old_factor.1, s32[4,8]{1,0:T(4,128)} %bitcast.3), custom_call_target="tpu_custom_call" | custom-call | tf_op jit(solution)/shard_map/pallas_call | solution.py:374
  83.3 0.0 copy-start
  83.3 2.4 %copy.10 = bf16[512,1024]{1,0:T(8,128)(2,1)} copy(bf16[512,1024]{1,0:T(8,128)(2,1)} %get-tuple-element.4) | data formatting | bytes 2097152
  85.8 0.0 copy-done
  85.8 1.3 %copy.11 = f32[1024,512]{1,0:T(8,128)} copy(f32[1024,512]{1,0:T(8,128)S(1)} %copy-done) | data formatting | bytes 4194304
Async XLA Ops:
  83.3 2.4 %copy-start = (f32[1024,512]{1,0:T(8,128)S(1)}, f32[1024,512]{1,0:T(8,128)}, u32[]{:S(2)}) copy-start(f32[1024,512]{1,0:T(8,128)} %get-tuple-element.5) | copy-start | bytes 6291460

commit v3 on v2

--- a/solution.py
+++ b/solution.py
@@ -142,8 +142,12 @@
             for i in (2 * h, 2 * h + 1):
                 arrived(rows.at[k, i, zh, y], turn_base + i)
             s["rows_z", h] = put(at, zh_mate)
-        s["rows", which, 1, h] = put(at, along_y(1))
-        s["rows", which, 3, h] = put(at, along_y(3))
+        if h:
+            s["rows", which, 3, 1] = put(at, along_y(3))
+            s["rows", which, 1, 1] = put(at, along_y(1))
+            s["rows", which, 3, 0] = put(group(which, y, 0), along_y(3))
+        else:
+            s["rows", which, 1, 0] = put(at, along_y(1))
 
     def rows_far(which, step):
         h = 0 if step == 1 else 1
@@ -153,6 +157,12 @@
     def rows_share(which, step):
         if step == 0:
             pass
+        elif step == 2 and which:
+            for way, h in ((1, 0), (3, 1)):
+                s["far", which, way].wait_recv()
+                at = group(which, ys(-step), h)
+                s["share", which, step, h] = put(at, sibling)
+            return
         elif step == 2:
             s["far", which, 1].wait_recv()
             s["far", which, 3].wait_recv()
@@ -161,11 +171,15 @@
         at = group(which, ys(-step))
         s["share", which, step] = put(at, sibling)
 
-    def dot(own, which, step):
+    def take(which, step):
+        if which and step == 2:
+            for h in (0, 1):
+                s["share", which, step, h].wait_recv()
+        else:
+            s["share", which, step].wait_recv()
+
+    def dot(own, zl_of, step):
         kk = k if own else 1 - k
-        zl_of = 1 - zh if which else zh
-        if not own:
-            s["share", which, step].wait_recv()
         q = ys(-step)
         stats[kk] += tdot(
             rows[kk, :, zl_of, q].reshape(512, 512), cols[:, zl_of, q].reshape(512, 512)
@@ -189,12 +203,11 @@
         s["cols", which, step, h].wait_recv()
         s["cols_far", which, step] = put(cols_half(which, -step, h), along_x(step))
 
-    def cols_all():
-        for which in (0, 1):
-            s["cols", which, 1, 1].wait_recv()
-            s["cols", which, 3, 0].wait_recv()
-            s["cols_far", which, 1].wait_recv()
-            s["cols_far", which, 3].wait_recv()
+    def cols_all(which):
+        s["cols", which, 1, 1].wait_recv()
+        s["cols", which, 3, 0].wait_recv()
+        s["cols_far", which, 1].wait_recv()
+        s["cols_far", which, 3].wait_recv()
 
     def part_sum():
         get_acts.wait()
@@ -344,14 +357,28 @@
     rows_share(0, 2)
     rows_share(1, 1)
     rows_share(1, 3)
-    cols_all()
-    for which, step in ((0, 0), (1, 0), (0, 1), (0, 3), (0, 2), (1, 1), (1, 3)):
-        dot(1, which, step)
-        dot(0, which, step)
+    cols_all(0)
+    take(0, 0)
+    take(1, 0)
+    dot(1, zl, 0)
+    dot(0, zl, 0)
+    for step in (1, 3):
+        take(0, step)
+        take(1, step)
+        dot(1, zl, step)
+        dot(0, zl, step)
     rows_share(1, 2)
-    dot(1, 1, 2)
+    cols_all(1)
+    for step in (0, 1, 3):
+        dot(1, 1 - zl, step)
+        dot(0, 1 - zl, step)
+    take(0, 2)
+    dot(1, zh, 2)
+    dot(0, zh, 2)
+    dot(1, 1 - zh, 2)
     blend(1)
-    dot(0, 1, 2)
+    take(1, 2)
+    dot(0, 1 - zh, 2)
     blend(0)
     result_end()
 

time: 87.2 us -> 84.2 us (0.966)
  Pallas kernels: 82.7 us -> 79.7 us
    pallas_call x1, Pallas kernels: 82.7 us -> 79.7 us  [local(): pl.pallas_call(kernel, out_shape=(jax.ShapeDtypeStruct((512, 1024), BF16)...]
where the time goes in v3:
time: 84.2 us; the launch traced here: 84.1 us
  Pallas kernels  79.7 us (95%)
  local copies, waits for them, and re-layouts  3.73 us (4%)
    pallas_call x1, Pallas kernels, local(): pl.pallas_call(kernel, out_shape=(jax.ShapeDtypeStruct((512, 1024), BF16)...  79.7 us
    unnamed x4, local copies, waits for them, and re-layouts  3.73 us

profile of v3, /device:TPU:1, one launch (start us, length us, event | category | flops | bytes accessed | tf_op | source)
XLA Modules:
  0.0 84.1 jit_solution(11395513413631501027)
XLA Ops:
  0.6 79.7 %shard_map.77 = (bf16[512,1024]{1,0:T(8,128)(2,1)}, f32[1024,512]{1,0:T(8,128)}) custom-call(bf16[4,128,512]{2,1,0:T(8,128)(2,1)} %bitcast.2, bf16[512,1024]{1,0:T(8,128)(2,1)} %out_grads.1, bf16[512,8192]{1,0:T(8,128)(2,1)} %codes.1, f32[4,64]{1,0:T(4,128)} %scales.1, f32[1024,512]{1,0:T(8,128)} %old_factor.1, s32[4,8]{1,0:T(4,128)} %bitcast.3), custom_call_target="tpu_custom_call" | custom-call | tf_op jit(solution)/shard_map/pallas_call | solution.py:401
  80.3 0.0 copy-start
  80.3 2.4 %copy.10 = bf16[512,1024]{1,0:T(8,128)(2,1)} copy(bf16[512,1024]{1,0:T(8,128)(2,1)} %get-tuple-element.4) | data formatting | bytes 2097152
  82.7 0.0 copy-done
  82.7 1.3 %copy.11 = f32[1024,512]{1,0:T(8,128)} copy(f32[1024,512]{1,0:T(8,128)S(1)} %copy-done) | data formatting | bytes 4194304
Async XLA Ops:
  80.3 2.4 %copy-start = (f32[1024,512]{1,0:T(8,128)S(1)}, f32[1024,512]{1,0:T(8,128)}, u32[]{:S(2)}) copy-start(f32[1024,512]{1,0:T(8,128)} %get-tuple-element.5) | copy-start | bytes 6291460

commit v4 on v3

--- a/solution.py
+++ b/solution.py
@@ -195,8 +195,12 @@
         if which and h == 0:
             s["cols_z"].wait_recv()
         at = cols_half(which, 0, h)
-        s["cols", which, 1, h] = put(at, along_x(1))
-        s["cols", which, 3, h] = put(at, along_x(3))
+        if h:
+            s["cols", which, 3, 1] = put(at, along_x(3))
+            s["cols", which, 1, 1] = put(at, along_x(1))
+            s["cols", which, 3, 0] = put(cols_half(which, 0, 0), along_x(3))
+        else:
+            s["cols", which, 1, 0] = put(at, along_x(1))
 
     def cols_far(step, which=0):
         h = 0 if step == 1 else 1

time: 84.2 us -> 84.2 us (level)
  no operation moved by 1% of the time
where the time goes in v4:
time: 84.2 us; the launch traced here: 84.1 us
  Pallas kernels  79.7 us (95%)
  local copies, waits for them, and re-layouts  3.73 us (4%)
    pallas_call x1, Pallas kernels, local(): pl.pallas_call(kernel, out_shape=(jax.ShapeDtypeStruct((512, 1024), BF16)...  79.7 us
    unnamed x4, local copies, waits for them, and re-layouts  3.73 us

profile of v4, /device:TPU:1, one launch (start us, length us, event | category | flops | bytes accessed | tf_op | source)
XLA Modules:
  0.0 84.1 jit_solution(7312873975433390295)
XLA Ops:
  0.6 79.7 %shard_map.77 = (bf16[512,1024]{1,0:T(8,128)(2,1)}, f32[1024,512]{1,0:T(8,128)}) custom-call(bf16[4,128,512]{2,1,0:T(8,128)(2,1)} %bitcast.2, bf16[512,1024]{1,0:T(8,128)(2,1)} %out_grads.1, bf16[512,8192]{1,0:T(8,128)(2,1)} %codes.1, f32[4,64]{1,0:T(4,128)} %scales.1, f32[1024,512]{1,0:T(8,128)} %old_factor.1, s32[4,8]{1,0:T(4,128)} %bitcast.3), custom_call_target="tpu_custom_call" | custom-call | tf_op jit(solution)/shard_map/pallas_call | solution.py:405
  80.3 0.0 copy-start
  80.3 2.4 %copy.10 = bf16[512,1024]{1,0:T(8,128)(2,1)} copy(bf16[512,1024]{1,0:T(8,128)(2,1)} %get-tuple-element.4) | data formatting | bytes 2097152
  82.7 0.0 copy-done
  82.7 1.3 %copy.11 = f32[1024,512]{1,0:T(8,128)} copy(f32[1024,512]{1,0:T(8,128)S(1)} %copy-done) | data formatting | bytes 4194304
Async XLA Ops:
  80.3 2.4 %copy-start = (f32[1024,512]{1,0:T(8,128)S(1)}, f32[1024,512]{1,0:T(8,128)}, u32[]{:S(2)}) copy-start(f32[1024,512]{1,0:T(8,128)} %get-tuple-element.5) | copy-start | bytes 6291460
